TPU v7x, 256 devices: a whole 4x4x8 slice. The times are simulated.
256 devices in a mesh: pa: 16 (over x, z_lo, core), pb: 16 (over y, z_hi).
Axes of the slice: x: 4, y: 4, z: 8 (z_hi: 4, z_lo: 2; z = z_hi * 2 + z_lo), core: 2. Of those that a mesh axis runs over, the one named last changes fastest.
Arguments:
- point_keys: bfloat16 [32768, 768], P(('pa', 'pb')), may hold values from -7 to 7
- point_values: bfloat16 [32768, 768], P(('pa', 'pb')), may hold values from -40 to 40
- out_grad: bfloat16 [32768, 768], P(('pa', 'pb')), may hold values from -512 to 512
- decoder_norm: float32 [12, 32768], P(None, ('pa', 'pb')), as said below
- latent_query: bfloat16 [1024, 768], P(('pa', 'pb')), may hold values from -4 to 4
- latent_out: bfloat16 [1024, 768], P(('pa', 'pb')), may hold values from -5 to 5
- encoder_norm: float32 [12, 1024], replicated, as said below
Outputs:
- keys_grad: bfloat16 [32768, 768], P(('pa', 'pb'))
- values_grad: bfloat16 [32768, 768], P(('pa', 'pb'))
- latent_grad: float32 [1024, 768], P(('pa', 'pb'))
Inputs may be any that keep to these rules, and one draw needn't show every extreme that they name: `decoder_norm`: each entry lies between log(1024) - 0.3 and log(1024) + 1.3. `encoder_norm`: each entry lies between log(32768) - 0.3 and log(32768) + 1.3.
All inputs are finite; a program needn't handle non-finite values.
Results may differ from a plain program's by a relative error of at most 0.004.
The roundings to bfloat16 on the way count: a program that leaves them out, or rounds other values in their place, can miss the bound.
Values may be sent and summed in bfloat16 or wider, within the bound.
A program may use at most 64 MiB of HBM per device.

v0:
```python
import jax
import jax.numpy as jnp
from jax import lax
from jax.sharding import PartitionSpec as P

HEADS = 12
HEAD_DIM = 64


def in_one_piece(arrays, axis, dim, along):
    widths = [a.shape[along] for a in arrays]
    both = jnp.concatenate(arrays, axis=along)
    result = lax.all_gather(both, axis, axis=dim, tiled=True)
    return tuple(jnp.split(result, [sum(widths[:k]) for k in range(1, len(widths))], axis=along))


def column(block, current):
    return lax.dynamic_slice_in_dim(block, current * HEAD_DIM, HEAD_DIM, 1)


def put_head(total, piece, current):
    return lax.dynamic_update_slice_in_dim(total, piece, current * HEAD_DIM, 1)


def add_head(total, piece, current):
    return put_head(total, column(total, current) + piece, current)


def across(left, right):
    return lax.dot_general(
        left, right, (((1,), (1,)), ((), ())), preferred_element_type=jnp.float32
    )


def down_rows(left, right):
    return lax.dot_general(
        left, right, (((0,), (0,)), ((), ())), preferred_element_type=jnp.float32
    )


def shards(
    point_keys, point_values, out_grad, decoder_norm, latent_query, latent_out, encoder_norm
):
    scale_factor = HEAD_DIM ** (-0.5)
    lat_all, out_all = in_one_piece((latent_query, latent_out), ("pa", "pb"), 0, 1)
    point_rows = point_keys.shape[0]
    latent_rows = lat_all.shape[0]
    width = point_keys.shape[1]

    def encoder_row(current):
        return lax.dynamic_slice_in_dim(encoder_norm, current, 1, 0)

    def pass_one(current, state):
        mix_acc, query_acc, key_acc, weighted_acc = state
        key_head = column(point_keys, current)
        grad_head = column(out_grad, current)
        lat_head = column(lat_all, current)
        scores = across(key_head, lat_head) * scale_factor
        decoder_weights = jnp.exp(scores - lax.dynamic_slice_in_dim(decoder_norm, current, 1, 0).T)
        decoder_gradient = across(grad_head, column(out_all, current))
        row_total = jnp.sum(decoder_weights * decoder_gradient, axis=1, keepdims=True)
        decoder_scores_grad = (decoder_weights * (decoder_gradient - row_total)).astype(
            jnp.bfloat16
        )
        mix_acc = put_head(
            mix_acc, down_rows(decoder_weights.astype(jnp.bfloat16), grad_head), current
        )
        query_acc = put_head(
            query_acc, down_rows(decoder_scores_grad, key_head) * scale_factor, current
        )
        key_acc = put_head(
            key_acc,
            jnp.dot(decoder_scores_grad, lat_head, preferred_element_type=jnp.float32)
            * scale_factor,
            current,
        )
        return (mix_acc, query_acc, key_acc, weighted_acc)

    weighted_blank = jnp.zeros((1, 1), jnp.float32)
    latent_blank = jnp.zeros((latent_rows, width), jnp.float32)
    begin = (
        latent_blank,
        latent_blank,
        jnp.zeros((point_rows, width), jnp.float32),
        weighted_blank,
    )
    mix_acc, query_acc, key_acc, weighted_acc = lax.fori_loop(0, HEADS, pass_one, begin)
    mix_grad = lax.psum(mix_acc, ("pa", "pb"))
    mixing_portion = mix_grad.astype(jnp.bfloat16)

    def pass_two(current, state):
        partial_rows, value_acc = state
        scores = across(column(point_keys, current), column(lat_all, current)) * scale_factor
        encoder_portion = jnp.exp(scores - encoder_row(current)).astype(jnp.bfloat16)
        mix_head = column(mixing_portion, current)
        encoder_gradient = across(column(point_values, current), mix_head)
        sums = jnp.sum(encoder_portion.astype(jnp.float32) * encoder_gradient, axis=0)[None, :]
        partial_rows = lax.dynamic_update_slice_in_dim(partial_rows, sums, current, 0)
        value_acc = put_head(
            value_acc,
            jnp.dot(encoder_portion, mix_head, preferred_element_type=jnp.float32),
            current,
        )
        return (partial_rows, value_acc)

    partial_rows, value_acc = lax.fori_loop(
        0,
        HEADS,
        pass_two,
        (jnp.zeros((HEADS, latent_rows), jnp.float32), jnp.zeros((point_rows, width), jnp.float32)),
    )
    column_total = lax.psum(partial_rows, ("pa", "pb"))

    def pass_three(current, state):
        query_acc, key_acc, value_acc = state
        key_head = column(point_keys, current)
        lat_head = column(lat_all, current)
        mix_head = column(mixing_portion, current)
        scores = across(key_head, lat_head) * scale_factor
        encoder = jnp.exp(scores - encoder_row(current))
        encoder_gradient = across(column(point_values, current), mix_head)
        encoder_scores_grad = (
            encoder * (encoder_gradient - lax.dynamic_slice_in_dim(column_total, current, 1, 0))
        ).astype(jnp.bfloat16)
        query_acc = add_head(
            query_acc, down_rows(encoder_scores_grad, key_head) * scale_factor, current
        )
        key_acc = add_head(
            key_acc,
            jnp.dot(encoder_scores_grad, lat_head, preferred_element_type=jnp.float32)
            * scale_factor,
            current,
        )
        return (query_acc, key_acc, value_acc)

    query_acc, key_acc, value_acc = lax.fori_loop(
        0, HEADS, pass_three, (query_acc, key_acc, value_acc)
    )
    latent_grad = lax.psum_scatter(query_acc, ("pa", "pb"), scatter_dimension=0, tiled=True)
    return (key_acc.astype(jnp.bfloat16), value_acc.astype(jnp.bfloat16), latent_grad)


def solution(mesh):
    in_specs = (
        P(("pa", "pb"), None),
        P(("pa", "pb"), None),
        P(("pa", "pb"), None),
        P(None, ("pa", "pb")),
        P(("pa", "pb"), None),
        P(("pa", "pb"), None),
        P(),
    )
    out_specs = (P(("pa", "pb"), None), P(("pa", "pb"), None), P(("pa", "pb"), None))
    return jax.shard_map(shards, mesh=mesh, in_specs=in_specs, out_specs=out_specs, check_vma=False)
```

profile of v0, /device:TPU:2, one launch (start us, length us, event | category | flops | bytes accessed | tf_op | source)
XLA Modules:
  0.0 1422.8 jit_solution(10542835375838273922)
XLA Ops:
  9.3 705.5 %all-gather.3.cloned.1.call-done = bf16[256,4,1536]{2,1,0:T(4,128)(2,1)} async-done(((bf16[1,4,1536]{2,1,0:T(4,128)(2,1)}), bf16[256,4,1536]{2,1,0:T(4,128)(2,1)}) %all-gather.3.cloned.1.call-update) | async-done | bytes 3145744 | tf_op jit(solution)/shard_map/all_gather | solution.py:13
  714.8 5.9 reshape.9
  720.7 2.1 fusion.49
  722.8 2.1 broadcast_in_dim.16
  724.9 2.1 broadcast_in_dim.16.clone
  727.0 84.2 %while.47 = (s32[]{:T(128)}, f32[1024,768]{0,1:T(8,128)}, f32[1024,768]{0,1:T(8,128)}, f32[128,768]{0,1:T(8,128)S(1)}, bf16[128,768]{1,0:T(8,128)(2,1)}, /*index...) while((s32[]{:T(128)}, f32[1024,768]{0,1:T(8,128)}, ...), condition=%wide.region_2.0_spmd, body=%wide.region_0.0_spmd.sunk | while | flops 85008256 | bytes 5414575 | solution.py:87
  730.1 1.8 fusion.96
  737.1 1.8 fusion.96
  738.9 1.8 convolution_dynamic-update-slice_fusion.4
  744.1 1.8 fusion.96
  745.8 1.8 convolution_dynamic-update-slice_fusion.4
  751.1 1.8 fusion.96
  752.9 1.8 convolution_dynamic-update-slice_fusion.4
  758.1 1.7 fusion.96
  759.9 1.8 convolution_dynamic-update-slice_fusion.4
  765.1 1.8 fusion.96
  766.9 1.8 convolution_dynamic-update-slice_fusion.4
  772.1 1.8 fusion.96
  773.9 1.8 convolution_dynamic-update-slice_fusion.4
  779.1 1.8 fusion.96
  780.9 1.8 convolution_dynamic-update-slice_fusion.4
  786.2 1.8 fusion.96
  787.9 1.8 convolution_dynamic-update-slice_fusion.4
  793.2 1.8 fusion.96
  795.0 1.8 convolution_dynamic-update-slice_fusion.4
  800.2 1.8 fusion.96
  802.0 1.8 convolution_dynamic-update-slice_fusion.4
  807.2 1.8 fusion.96
  809.0 1.8 convolution_dynamic-update-slice_fusion.4
  811.1 3.6 copy.14
  814.7 131.6 %all-reduce.5 = bf16[1024,768]{1,0:T(8,128)(2,1)S(1)} all-reduce(f32[1024,768]{1,0:T(8,128)} %copy.14), channel_id=1, replica_groups=mesh['pa'=16,'pb'=16] {'pa','pb'}, use_global_device_ids=true, to_apply=%region_3.0 | all-reduce | flops 786432 | bytes 4718592 | tf_op jit(solution)/shard_map/psum | solution.py:88
  946.3 64.0 %while.48 = (s32[]{:T(128)}, f32[12,1024]{1,0:T(8,128)}, bf16[128,768]{0,1:T(8,128)(2,1)}, bf16[128,768]{1,0:T(8,128)(2,1)}, bf16[1024,768]{1,0:T(8,128)(2,1)S(1...) while((s32[]{:T(128)}, f32[12,1024]{1,0:T(8,128)}, ...), condition=%wide.region_6.0_spmd, body=%wide.region_4.0_spmd.sunk | while | flops 51117060 | bytes 1698987 | solution.py:106
  1010.3 74.3 %psum.15 = f32[12,1024]{1,0:T(8,128)} all-reduce(f32[12,1024]{1,0:T(8,128)} %get-tuple-element.457), channel_id=1, replica_groups=mesh['pa'=16,'pb'=16] {'pa','pb'}, use_global_device_ids=true, to_apply=%region_7.0 | all-reduce | flops 12288 | bytes 98304 | tf_op jit(solution)/shard_map/psum | solution.py:112
  1084.6 64.4 %while.49 = (s32[]{:T(128)}, f32[1024,768]{0,1:T(8,128)}, f32[128,768]{0,1:T(8,128)S(1)}, bf16[128,768]{1,0:T(8,128)(2,1)}, bf16[1024,768]{1,0:T(8,128)(2,1)S(1)...) while((s32[]{:T(128)}, f32[1024,768]{0,1:T(8,128)}, ...), condition=%wide.region_9.0_spmd, body=%wide.region_8.0_spmd.sunk | while | flops 67911680 | bytes 3338415 | solution.py:136
  1087.6 2.0 fusion.115
  1092.9 2.0 fusion.115
  1098.3 2.0 fusion.115
  1103.7 2.0 fusion.115
  1109.0 2.0 fusion.115
  1114.4 2.0 fusion.115
  1119.7 2.0 fusion.115
  1125.1 2.0 fusion.115
  1130.5 2.0 fusion.115
  1135.9 2.0 fusion.115
  1141.2 2.0 fusion.115
  1146.6 2.0 fusion.115
  1149.0 3.6 copy.17
  1154.3 260.3 %all-reduce.4.cloned.1.call-done = f32[1024,768]{1,0:T(8,128)} async-done(((f32[1024,768]{1,0:T(8,128)}), f32[1024,768]{1,0:T(8,128)}) %all-reduce.4.cloned.1.call-update) | async-done | bytes 3145744
  (182 shorter events, 152.0 us)
Async XLA Ops:
  7.2 707.6 %all-gather.3.cloned.1.call-start = ((), (), s32[]{:S(2)}) async-start(), calls=%async_computation | async-start | bytes 3158016 | tf_op jit(solution)/shard_map/all_gather | solution.py:13
  8.6 1406.0 %all-reduce.4.cloned.1.call-start = ((), (), s32[]{:S(2)}) async-start(), calls=%async_computation.1 | async-start | bytes 6291456
  1152.5 0.9 copy-start
Sparse Core Ops, SparseCore 0:
  10.4 704.3 all-gather.2
  1152.7 261.8 all-reduce.3
where the time goes:
time: 1430 us; the launch traced here: 1420 us
  waiting for transfers between devices  966 us (68%)
  blocking collectives  206 us (14%)
  matrix products  166 us (12%)
  local copies, waits for them, and re-layouts  66.2 us (5%)
    all_gather x1, waiting for transfers between devices, in_one_piece(): result = lax.all_gather(both, axis, axis=dim, tiled=True)  706 us
    unnamed x3, waiting for transfers between devices  260 us
    psum x1, blocking collectives, shards(): mix_grad = lax.psum(mix_acc, ('pa', 'pb'))  132 us
    dot_general x72, matrix products, across(): lax.dot_general(left, right, (((1,), (1,)), ((), ())), preferred_element_...  79.1 us
    psum x1, blocking collectives, shards(): column_total = lax.psum(partial_rows, ('pa', 'pb'))  74.3 us
    dot_general x36, matrix products, down_rows(): lax.dot_general(left, right, (((0,), (0,)), ((), ())), preferred_element_...  66.2 us
  transfers between devices with their start and end apart: 2, of which 2 were waited for; matrix products, arithmetic and copies ran while one was open for 0% of the time, Pallas kernels for 0%

commit v1 on v0

--- a/solution.py
+++ b/solution.py
@@ -109,7 +109,7 @@
         pass_two,
         (jnp.zeros((HEADS, latent_rows), jnp.float32), jnp.zeros((point_rows, width), jnp.float32)),
     )
-    column_total = lax.psum(partial_rows, ("pa", "pb"))
+    column_total = jnp.sum(lax.all_gather(partial_rows, ("pa", "pb")), axis=0)
 
     def pass_three(current, state):
         query_acc, key_acc, value_acc = state

time: 1430 us -> 2100 us (1.47)
  waiting for transfers between devices: 966 us -> 1700 us
  blocking collectives: 206 us -> 132 us
    all_gather x0 -> x1, waiting for transfers between devices: none -> 727 us  [shards(): column_total = jnp.sum(lax.all_gather(partial_rows, ('pa', 'pb')), axis=0)]
    psum x1 -> x0, blocking collectives: 74.3 us -> none  [shards(): column_total = lax.psum(partial_rows, ('pa', 'pb'))]
    unnamed x3 -> x4, waiting for transfers between devices: 260 us -> 264 us
  transfers between devices with their start and end apart: 2 -> 3, of which waited for: 2 -> 3; matrix products, arithmetic and copies ran while one was open for 0% -> 0% of each run, Pallas kernels for 0% -> 0%
where the time goes in v1:
time: 2100 us; the launch traced here: 2090 us
  waiting for transfers between devices  1700 us (81%)
  matrix products  169 us (8%)
  blocking collectives  132 us (6%)
  local copies, waits for them, and re-layouts  68 us (3%)
    all_gather x1, waiting for transfers between devices, shards(): column_total = jnp.sum(lax.all_gather(partial_rows, ('pa', 'pb')), axis=0)  727 us
    all_gather x1, waiting for transfers between devices, in_one_piece(): result = lax.all_gather(both, axis, axis=dim, tiled=True)  706 us
    unnamed x4, waiting for transfers between devices  264 us
    psum x1, blocking collectives, shards(): mix_grad = lax.psum(mix_acc, ('pa', 'pb'))  132 us
    dot_general x72, matrix products, across(): lax.dot_general(left, right, (((1,), (1,)), ((), ())), preferred_element_...  81.6 us
    dot_general x36, matrix products, down_rows(): lax.dot_general(left, right, (((0,), (0,)), ((), ())), preferred_element_...  66.2 us
  transfers between devices with their start and end apart: 3, of which 3 were waited for; matrix products, arithmetic and copies ran while one was open for 0% of the time, Pallas kernels for 0%

profile of v1, /device:TPU:2, one launch (start us, length us, event | category | flops | bytes accessed | tf_op | source)
XLA Modules:
  0.0 2090.5 jit_solution(11692065867671285971)
XLA Ops:
  9.3 705.5 %all-gather.6.cloned.1.call-done = bf16[256,4,1536]{2,1,0:T(4,128)(2,1)} async-done(((bf16[1,4,1536]{2,1,0:T(4,128)(2,1)}), bf16[256,4,1536]{2,1,0:T(4,128)(2,1)}) %all-gather.6.cloned.1.call-update) | async-done | bytes 3145744 | tf_op jit(solution)/shard_map/all_gather | solution.py:13
  714.8 5.9 reshape.10
  720.7 3.2 fusion.49
  723.9 2.0 broadcast_in_dim.16
  726.0 2.0 broadcast_in_dim.16.clone
  728.1 86.7 %while.47 = (s32[]{:T(128)}, f32[1024,768]{0,1:T(8,128)}, f32[1024,768]{0,1:T(8,128)}, f32[128,768]{0,1:T(8,128)S(1)}, bf16[128,768]{1,0:T(8,128)(2,1)}, /*index...) while((s32[]{:T(128)}, f32[1024,768]{0,1:T(8,128)}, ...), condition=%wide.region_2.0_spmd, body=%wide.region_0.0_spmd.sunk | while | flops 85008256 | bytes 5414575 | solution.py:87
  731.4 1.8 fusion.96
  738.6 1.8 fusion.96
  740.3 1.7 convolution_dynamic-update-slice_fusion.4
  745.8 1.8 fusion.96
  752.9 1.8 fusion.96
  754.7 1.8 convolution_dynamic-update-slice_fusion.4
  760.2 1.8 fusion.96
  761.9 1.8 convolution_dynamic-update-slice_fusion.4
  767.4 1.8 fusion.96
  769.2 1.8 convolution_dynamic-update-slice_fusion.4
  774.6 1.8 fusion.96
  776.4 1.7 convolution_dynamic-update-slice_fusion.4
  781.9 1.8 fusion.96
  783.6 1.8 convolution_dynamic-update-slice_fusion.4
  789.1 1.8 fusion.96
  790.9 1.8 convolution_dynamic-update-slice_fusion.4
  796.3 1.8 fusion.96
  798.1 1.8 convolution_dynamic-update-slice_fusion.4
  803.6 1.8 fusion.96
  805.3 1.8 convolution_dynamic-update-slice_fusion.4
  810.8 1.8 fusion.96
  812.6 1.8 convolution_dynamic-update-slice_fusion.4
  814.7 3.6 copy.14
  818.3 131.5 %all-reduce.5 = bf16[1024,768]{1,0:T(8,128)(2,1)S(1)} all-reduce(f32[1024,768]{1,0:T(8,128)} %copy.14), channel_id=1, replica_groups=mesh['pa'=16,'pb'=16] {'pa','pb'}, use_global_device_ids=true, to_apply=%region_3.0 | all-reduce | flops 786432 | bytes 4718592 | tf_op jit(solution)/shard_map/psum | solution.py:88
  949.8 64.0 %while.48 = (s32[]{:T(128)}, f32[12,1024]{1,0:T(8,128)}, bf16[128,768]{0,1:T(8,128)(2,1)}, bf16[128,768]{1,0:T(8,128)(2,1)}, bf16[1024,768]{1,0:T(8,128)(2,1)S(1...) while((s32[]{:T(128)}, f32[12,1024]{1,0:T(8,128)}, ...), condition=%wide.region_6.0_spmd, body=%wide.region_4.0_spmd.sunk | while | flops 51117060 | bytes 1698987 | solution.py:106
  1013.9 726.6 %all-gather.8.cloned.1.call-done = f32[256,12,1024]{2,1,0:T(8,128)} async-done(((f32[1,12,1024]{2,1,0:T(8,128)}), f32[256,12,1024]{2,1,0:T(8,128)}) %all-gather.8.cloned.1.call-update) | async-done | bytes 12582928 | tf_op jit(solution)/shard_map/all_gather | solution.py:112
  1740.5 7.3 reduce_sum.35
  1747.9 64.4 %while.49 = (s32[]{:T(128)}, f32[1024,768]{0,1:T(8,128)}, f32[128,768]{0,1:T(8,128)S(1)}, bf16[128,768]{1,0:T(8,128)(2,1)}, bf16[1024,768]{1,0:T(8,128)(2,1)S(1)...) while((s32[]{:T(128)}, f32[1024,768]{0,1:T(8,128)}, ...), condition=%wide.region_9.0_spmd, body=%wide.region_8.0_spmd.sunk | while | flops 67911680 | bytes 3338415 | solution.py:136
  1750.9 2.0 fusion.115
  1756.2 2.0 fusion.115
  1761.6 2.0 fusion.115
  1766.9 2.0 fusion.115
  1772.3 2.0 fusion.115
  1777.7 2.0 fusion.115
  1783.1 2.0 fusion.115
  1788.4 2.0 fusion.115
  1793.8 2.0 fusion.115
  1799.2 2.0 fusion.115
  1804.5 2.0 fusion.115
  1809.9 2.0 fusion.115
  1812.3 3.5 copy.17
  1818.4 264.2 %all-reduce.4.cloned.1.call-done = f32[1024,768]{1,0:T(8,128)} async-done(((f32[1024,768]{1,0:T(8,128)}), f32[1024,768]{1,0:T(8,128)}) %all-reduce.4.cloned.1.call-update) | async-done | bytes 3145744
  (185 shorter events, 157.2 us)
Async XLA Ops:
  7.2 707.6 %all-gather.6.cloned.1.call-start = ((), (), s32[]{:S(2)}) async-start(), calls=%async_computation | async-start | bytes 3158016 | tf_op jit(solution)/shard_map/all_gather | solution.py:13
  8.6 1732.0 %all-gather.8.cloned.1.call-start = ((), (), s32[]{:S(2)}) async-start(), calls=%async_computation.1 | async-start | bytes 16842752 | tf_op jit(solution)/shard_map/all_gather | solution.py:112
  1013.9 1068.8 %all-reduce.4.cloned.1.call-start = ((), (), s32[]{:S(2)}) async-start(), calls=%async_computation.2 | async-start | bytes 6291456
  1815.9 0.9 copy-start
Sparse Core Ops, SparseCore 0:
  10.4 704.3 all-gather.5
  1014.0 726.5 all-gather.7
  1816.0 266.5 all-reduce.3
